TPU v7x, 256 devices: a whole 4x4x8 slice. The times are simulated.
256 devices in a mesh: dp: 32 (over x, y, core), tensor: 8 (over z).
Axes of the slice: x: 4, y: 4, z: 8, core: 2. Of those that a mesh axis runs over, the one named last changes fastest.
Arguments:
- queries: bfloat16 [16384, 8192], P('dp', 'tensor'), may hold values from -8 to 8
- suffix_kv: bfloat16 [16384, 2048], P('dp', 'tensor'), may hold values from -8 to 8
- prefix_key_value: bfloat16 [256, 64, 2048], P('dp', None, 'tensor'), may hold values from -5 to 5
- answer_ids: int32 [32, 512], P('dp'), may hold values from 0 to 15, never falling along the last dimension, each value on 1 to 64 neighbouring positions
- read_tiles: int32 [32, 26], P('dp'), may hold values from 0 to 255, as said below
- visible: int32 [32, 2, 26], P('dp'), may hold values 0 or 1
- out_weight: bfloat16 [8192, 4096], P('tensor', 'dp'), may hold values from -0.1875 to 0.1875
Outputs:
- scored: bfloat16 [16384, 4096], P('dp', 'tensor')
Inputs may be any that keep to these rules, and one draw needn't show every extreme that they name: `answer_ids`: along a row answer numbers never fall; each answer has 1 to 64 tokens, and some answer has exactly that many. `read_tiles`: tile t is stored by data group t // 8. A row lists 26 distinct tiles in no fixed order. The same 2 tiles, stored by one data group, stand in every row; of the other tiles of a row at most one is stored by any one data group.
All inputs are finite; a program needn't handle non-finite values. No bound on the sum of `visible` on one device may be relied on, other than what follows from the above.
Results may differ from a plain program's by a relative error of at most 0.0052.
Values may be sent and summed in bfloat16 or wider, within the bound.
A program may use at most 64 MiB of HBM per device.

v0:
```python
import jax
import jax.numpy as jnp
from jax import lax
from jax.sharding import PartitionSpec as P

HEAD_WIDTH = 128
ANS_DEV = 16
QG = 2


def head_attention(head_query, head_keys, head_values, visible_keys):
    scores = jnp.dot(head_query, head_keys.T, preferred_element_type=jnp.float32) * HEAD_WIDTH ** (
        -0.5
    )
    scores = jnp.where(visible_keys, scores, -jnp.inf)
    row_max = jnp.max(scores, axis=1, keepdims=True)
    exponent = jnp.exp(scores - row_max)
    row_total = jnp.sum(exponent, axis=1, keepdims=True)
    weights = exponent.astype(jnp.bfloat16)
    mixed = jnp.dot(weights, head_values, preferred_element_type=jnp.float32)
    return (mixed / row_total).astype(jnp.bfloat16)


def local(queries, suffix_kv, prefix_key_value, answer_ids, read_tiles, visible, out_weight):
    tile_len = prefix_key_value.shape[1]
    row_width = prefix_key_value.shape[2]
    my_reads = read_tiles[0]
    blank_tiles = jnp.zeros((my_reads.shape[0], tile_len, row_width), prefix_key_value.dtype)
    column_block = lax.all_gather(prefix_key_value, "dp", axis=0, tiled=True)
    present = (my_reads >= 0) & (my_reads < column_block.shape[0])
    fetched = jnp.take(column_block, jnp.clip(my_reads, 0, column_block.shape[0] - 1), axis=0)
    gathered_tiles = jnp.where(present[:, None, None], fetched, blank_tiles)
    token_count = queries.shape[0]
    heads_here = queries.shape[1] // HEAD_WIDTH
    kv_here = suffix_kv.shape[1] // (2 * HEAD_WIDTH)
    answer_of = answer_ids[0]
    question_of = answer_of * QG // ANS_DEV
    question_hit = question_of[:, None] == jnp.arange(QG, dtype=jnp.int32)[None, :]
    seen = jnp.any(question_hit[:, :, None] & (visible[0][None, :, :] > 0), axis=1)
    prefix_mask = jnp.repeat(seen, tile_len, axis=1)
    position = jnp.arange(token_count, dtype=jnp.int32)
    suffix_mask = (answer_of[:, None] == answer_of[None, :]) & (
        position[:, None] >= position[None, :]
    )
    visible_keys = jnp.concatenate([prefix_mask, suffix_mask], axis=1)
    key_value_pairs = jnp.concatenate([gathered_tiles.reshape(-1, row_width), suffix_kv], axis=0)
    key_value_pairs = key_value_pairs.reshape(-1, kv_here, 2, HEAD_WIDTH)
    per_head = queries.reshape(token_count, heads_here, HEAD_WIDTH).transpose(1, 0, 2)
    heads_per_group = heads_here // kv_here

    def one_head(packed):
        head_index, head_query = packed
        key_value = lax.dynamic_index_in_dim(
            key_value_pairs, head_index // heads_per_group, 1, keepdims=False
        )
        return head_attention(head_query, key_value[:, 0], key_value[:, 1], visible_keys)

    heads_out = lax.map(one_head, (jnp.arange(heads_here, dtype=jnp.int32), per_head))
    attended = heads_out.transpose(1, 0, 2).reshape(token_count, heads_here * HEAD_WIDTH)
    partial_terms = jnp.dot(
        attended,
        lax.all_gather(out_weight, "dp", axis=1, tiled=True),
        preferred_element_type=jnp.float32,
    )
    return lax.psum_scatter(partial_terms, "tensor", scatter_dimension=1, tiled=True).astype(
        jnp.bfloat16
    )


def solution(mesh):
    placed = (
        P("dp", "tensor"),
        P("dp", "tensor"),
        P("dp", None, "tensor"),
        P("dp", None),
        P("dp", None),
        P("dp", None, None),
        P("tensor", "dp"),
    )
    return jax.shard_map(
        local, mesh=mesh, in_specs=placed, out_specs=P("dp", "tensor"), check_vma=False
    )
```

profile of v0, /device:TPU:1, one launch (start us, length us, event | category | flops | bytes accessed | tf_op | source)
XLA Modules:
  0.0 252.0 jit_solution(2097175696983329573)
XLA Ops:
  9.7 1.1 copy.27
  12.5 1.0 fusion.18
  13.8 1.2 copy.31
  15.0 1.3 copy.26
  16.4 55.7 %all-gather.3.cloned.1.call-done = bf16[256,64,256]{2,1,0:T(8,128)(2,1)} async-done(((bf16[8,64,256]{2,1,0:T(8,128)(2,1)}), bf16[256,64,256]{2,1,0:T(8,128)(2,1)}) %all-gather.3.cloned.1.call-update) | async-done | bytes 8388624 | tf_op jit(solution)/shard_map/all_gather | solution.py:29
  72.1 4.0 %gather_fusion = bf16[26,64,256]{2,1,0:T(8,128)(2,1)S(1)} fusion(bf16[256,64,256]{2,1,0:T(8,128)(2,1)} %all-gather.3.cloned.1.call-done, s32[1024]{0:T(1024)S(1)} %pad_clamp_fusion), kind=kCustom, calls=%fused_computation | custom fusion | bytes 1704040 | tf_op jit(solution)/shard_map/jit(_take)/gather | solution.py:31
  76.3 8.1 %broadcast_select_fusion.1 = bf16[1664,1,2,128]{3,2,0,1:T(2,128)(2,1)S(1)} fusion(pred[1664]{0:T(1024)(128)(4,1)S(1)} %broadcast_in_dim.55, bf16[1664,1,2,128]{3,2,0,1:T(2,128)(2,1)S(1)} %gather.7, pred[1664]{0:T(1024)(128)(4,1)S(1)} %broadcast_in_dim.58), kind=kLoop, calls=%fused_computation.19 | loop fusion | flops 851968 | bytes 1707264 | tf_op jit(solution)/shard_map/jit(_where)/select_n | solution.py:32
  84.4 9.7 %pad_maximum_fusion = bf16[2176,1,2,128]{3,2,0,1:T(2,128)(2,1)S(1)} fusion(bf16[512,1,2,128]{3,2,0,1:T(2,128)(2,1)S(1)} %copy.28, bf16[1664,1,2,128]{3,2,0,1:T(2,128)(2,1)S(1)} %broadcast_select_fusion.1), kind=kLoop, calls=%fused_computation.20 | loop fusion | flops 557056 | bytes 2228224 | tf_op jit(solution)/shard_map/concatenate | solution.py:46
  94.3 30.1 %while.11 = (s32[]{:T(128)}, bf16[8,512,128]{1,2,0:T(8,128)(2,1)S(1)}, bf16[8,512,128]{1,2,0:T(8,128)(2,1)}, bf16[2176,1,2,128]{3,0,2,1:T(8,128)(2,1)S(1)}, pred[512,2176]{1,0:T(32,128)(4,1)S(1)}, /*index=5*/s32[]{:T(128)}) while((s32[]{:T(128)}, bf16[8,512,128]{1,2,0:T(8,128)(2,1)S(1)}, bf16[8,512,128]{1,2,0:T(8,128)(2,1)}, ...), condition=%wide.region_4.5_spmd, body=%wide.region_1.4_spmd.sunk | while | flops 578354176 | bytes 16394325 | solution.py:58
  94.3 2.0 fusion.31
  97.1 0.8 fusion.33
  98.1 2.0 fusion.31
  101.9 2.0 fusion.31
  105.6 2.0 fusion.31
  108.4 0.8 fusion.33
  109.4 2.0 fusion.31
  113.2 2.0 fusion.31
  115.9 0.8 fusion.33
  116.9 2.0 fusion.31
  120.7 2.0 fusion.31
  124.5 14.5 %all-gather.5.cloned.1.call-done = bf16[1024,4096]{1,0:T(8,128)(2,1)} async-done(((bf16[1024,128]{1,0:T(8,128)(2,1)}), bf16[1024,4096]{1,0:T(8,128)(2,1)}) %all-gather.5.cloned.1.call-update) | async-done | bytes 8388624 | tf_op jit(solution)/shard_map/all_gather | solution.py:62
  139.0 10.1 %fusion.23 = f32[512,4096]{1,0:T(8,128)} fusion(bf16[512,1024]{0,1:T(8,128)(2,1)S(1)} %bitcast.52, bf16[1024,4096]{1,0:T(8,128)(2,1)} %all-gather.5.cloned.1.call-done), kind=kOutput, calls=%fused_computation.40 | convolution fusion | flops 4294967296 | bytes 17825792 | tf_op jit(solution)/shard_map/dot_general | solution.py:60
  149.1 94.3 %reduce-scatter.2.cloned.1.call-done = f32[512,512]{1,0:T(8,128)} async-done(((f32[512,4096]{1,0:T(8,128)}), f32[512,512]{1,0:T(8,128)}) %reduce-scatter.2.cloned.1.call-update) | async-done | bytes 1048592 | tf_op jit(solution)/shard_map/reduce_scatter | solution.py:65
  243.4 2.1 convert_element_type.11
  (59 shorter events, 16.6 us)
Async XLA Ops:
  6.5 8.5 %copy-start.1 = (bf16[512,1024]{1,0:T(8,128)(2,1)S(1)}, bf16[512,1024]{1,0:T(8,128)(2,1)}, u32[]{:S(2)}) copy-start(bf16[512,1024]{1,0:T(8,128)(2,1)} %param.9) | copy-start | bytes 3145732
  6.5 65.5 %all-gather.3.cloned.1.call-start = ((), (), s32[]{:S(2)}) async-start(), calls=%async_computation.1 | async-start | bytes 8650752 | tf_op jit(solution)/shard_map/all_gather | solution.py:29
  7.3 131.7 %all-gather.5.cloned.1.call-start = ((), (), s32[]{:S(2)}) async-start(), calls=%async_computation.2 | async-start | bytes 8650752 | tf_op jit(solution)/shard_map/all_gather | solution.py:62
  8.0 8.3 %copy-start.2 = (s32[1,26]{1,0:T(1,128)S(1)}, s32[1,26]{1,0:T(1,128)}, u32[]{:S(2)}) copy-start(s32[1,26]{1,0:T(1,128)} %param.13) | copy-start | bytes 316
  8.0 235.4 %reduce-scatter.2.cloned.1.call-start = ((), (), s32[]{:S(2)}) async-start(), calls=%async_computation.3 | async-start | bytes 9437184 | tf_op jit(solution)/shard_map/reduce_scatter | solution.py:65
  84.4 9.9 %copy-start = (bf16[8,512,128]{1,2,0:T(8,128)(2,1)S(1)}, bf16[8,512,128]{1,2,0:T(8,128)(2,1)}, u32[]{:S(2)}) copy-start(bf16[8,512,128]{1,2,0:T(8,128)(2,1)} %custom-call.2) | copy-start | bytes 3145732
Sparse Core Ops, SparseCore 0:
  9.9 62.1 all-gather.2
  74.5 64.3 all-gather.4
  149.3 94.1 reduce-scatter.1
where the time goes:
time: 252 us
  waiting for transfers between devices  166 us (66%)
  matrix products  33 us (13%)
  other arithmetic  29.7 us (12%)
  between operations  13.3 us (5%)
  local copies, waits for them, and re-layouts  9.73 us (4%)
    reduce_scatter x1, waiting for transfers between devices, local(): lax.psum_scatter(partial_terms, 'tensor', scatter_dimension=1, tiled=True)  94.3 us
    all_gather x1, waiting for transfers between devices, local(): column_block = lax.all_gather(prefix_key_value, 'dp', axis=0, tiled=True)  55.7 us
    dot_general x8, matrix products, head_attention(): jnp.dot(head_query, head_keys.T, preferred_element_type=jnp.float32)  16.3 us
    all_gather x1, waiting for transfers between devices, local(): lax.all_gather(out_weight, 'dp', axis=1, tiled=True)  14.5 us
    dot_general x1, matrix products, local(): jnp.dot(attended, lax.all_gather(out_weight, 'dp', axis=1, tiled=True), p...  10.1 us
    concatenate x1, other arithmetic, local(): jnp.concatenate([gathered_tiles.reshape(-1, row_width), suffix_kv], axis=0)  9.72 us
    select_n x1, other arithmetic, local(): gathered_tiles = jnp.where(present[:, None, None], fetched, blank_tiles)  8.13 us
    dot_general x8, matrix products, head_attention(): mixed = jnp.dot(weights, head_values, preferred_element_type=jnp.float32)  6.58 us
  transfers between devices with their start and end apart: 3, of which 3 were waited for; matrix products, arithmetic and copies ran while one was open for 24% of the time, Pallas kernels for 0%

commit v1 on v0

v1 whole, which is shorter than its diff:
```python
import functools

import jax
import jax.numpy as jnp
from jax import lax
from jax.experimental import pallas as pl
from jax.experimental.pallas import tpu as pltpu
from jax.sharding import PartitionSpec as P

HEAD = 128
TILE = 64
READS = 26
GROUPS = 32
TPS = 8
TOK = 512
HEADS = 8
BLK = 128
NBLK = TOK // BLK
PRE = READS * TILE
KEYS = PRE + 2 * BLK
NZ = 8
COLS = 512
MESH = pl.DeviceIdType.MESH
BIG = -1e30
LOG2E = 1.4426950408889634
SCALE = HEAD ** (-0.5) * LOG2E


def coords():
    g = lax.axis_index("dp")
    return g // 8, lax.rem(g // 2, 4), lax.rem(g, 2), lax.axis_index("tensor")


def place(x, y, c):
    return lax.rem(x, 4) * 8 + lax.rem(y, 4) * 2 + lax.rem(c, 2)


def remote(src, dst, send, recv, dp, tensor):
    return pltpu.make_async_remote_copy(
        src_ref=src, dst_ref=dst, send_sem=send, recv_sem=recv,
        device_id=(dp, tensor), device_id_type=MESH,
    )


def fetch_kernel(reads, prefix, keys, values, ask, table, asked, packed, got,
                 hot_out, sem_send, sem_recv, hot_recv, spread_send, spread_recv, local_sem):
    x, y, c, z = coords()
    me = lax.axis_index("dp")
    peers = [place(x + k // 8, y + (k // 2) % 4, c + k % 2) for k in range(1, GROUPS)]
    barrier = pltpu.get_barrier_semaphore()
    for peer in peers:
        pl.semaphore_signal(barrier, inc=1, device_id=(peer, z), device_id_type=MESH)

    lane = lax.broadcasted_iota(jnp.int32, (1, 128), 1)
    first = jnp.full((1, 128), TPS, jnp.int32)
    last = jnp.full((1, 128), -1, jnp.int32)
    tiles = [reads[0, r] for r in range(READS)]
    for tile in tiles:
        here = lane == tile // TPS
        first = jnp.where(here, jnp.minimum(first, tile % TPS), first)
        last = jnp.where(here, jnp.maximum(last, tile % TPS), last)
    twice = last > first
    hot_owner = jnp.max(jnp.where(twice, lane, 0))
    hot_second = jnp.max(jnp.where(twice, last, 0))
    mine = jnp.where(first == TPS, 0, first)
    ask[...] = mine
    table[pl.ds(me, 1)] = mine[None]
    second = prefix[hot_second]
    hot_out[pl.ds(0, TILE)] = second[:, :HEAD]
    hot_out[pl.ds(TILE, TILE)] = second[:, HEAD:]

    pl.semaphore_wait(barrier, GROUPS - 1)
    for peer in peers:
        remote(ask, table.at[me], sem_send.at[0], sem_recv.at[0], peer, z).start()
    for peer in peers:
        part = pl.multiple_of(lax.rem(peer, 8) * 16, 16)
        remote(hot_out.at[pl.ds(part, 16)], hot_recv.at[me],
               sem_send.at[1], sem_recv.at[1], peer, z).start()
    my_part = pl.multiple_of(lax.rem(me, 8) * 16, 16)
    hot_recv[pl.ds(me, 1)] = hot_out[pl.ds(my_part, 16)][None]

    others = table.at[pl.ds(0, GROUPS - 1)]
    pltpu.make_async_copy(others, others, sem_recv.at[0]).wait()
    load = pltpu.make_async_copy(table, asked, local_sem)
    load.start()
    load.wait()
    for k, peer in enumerate(peers):
        tile = prefix[asked[peer, 0, me]]
        packed[k, pl.ds(0, TILE)] = tile[:, :HEAD]
        packed[k, pl.ds(TILE, TILE)] = tile[:, HEAD:]
        remote(packed.at[k], got.at[me], sem_send.at[2], sem_recv.at[2], peer, z).start()
    own = prefix[asked[me, 0, me]]
    got[pl.ds(me, 1), pl.ds(0, TILE)] = own[:, :HEAD][None]
    got[pl.ds(me, 1), pl.ds(TILE, TILE)] = own[:, HEAD:][None]

    others = hot_recv.at[pl.ds(0, GROUPS - 1)]
    pltpu.make_async_copy(others, others, sem_recv.at[1]).wait()
    piece = hot_recv[hot_owner]
    got[GROUPS, pl.ds(my_part, 16)] = piece
    spread = []
    for k in range(1, 8):
        peer = place(x, y + k // 2, c + k % 2)
        copy = remote(got.at[GROUPS, pl.ds(my_part, 16)], got.at[GROUPS, pl.ds(my_part, 16)],
                      spread_send.at[k], spread_recv.at[k], peer, z)
        copy.start()
        spread.append(copy)

    others = got.at[pl.ds(0, GROUPS - 1)]
    pltpu.make_async_copy(others, others, sem_recv.at[2]).wait()
    for copy in spread:
        copy.wait_recv()
    for r, tile in enumerate(tiles):
        owner = tile // TPS
        from_second = (owner == hot_owner) & (tile % TPS == hot_second)
        block = got[jnp.where(from_second, GROUPS, owner)]
        keys[pl.ds(r * TILE, TILE)] = block[:TILE]
        values[pl.ds(r * TILE, TILE)] = block[TILE:]
    for ref, sem in ((table.at[pl.ds(0, GROUPS - 1)], sem_send.at[0]),
                     (hot_recv.at[pl.ds(0, GROUPS - 1)], sem_send.at[1]),
                     (packed, sem_send.at[2])):
        pltpu.make_async_copy(ref, ref, sem).wait()
    for copy in spread:
        copy.wait_send()


def fetch(reads, prefix):
    half = jax.ShapeDtypeStruct((PRE, HEAD), jnp.bfloat16)
    vmem = pl.BlockSpec(memory_space=pltpu.VMEM)
    return pl.pallas_call(
        fetch_kernel,
        out_shape=(half, half),
        in_specs=[pl.BlockSpec(memory_space=pltpu.SMEM), vmem],
        out_specs=(vmem, vmem),
        scratch_shapes=[
            pltpu.VMEM((1, 128), jnp.int32),
            pltpu.VMEM((GROUPS, 1, 128), jnp.int32),
            pltpu.SMEM((GROUPS, 1, 128), jnp.int32),
            pltpu.VMEM((GROUPS - 1, 2 * TILE, HEAD), jnp.bfloat16),
            pltpu.VMEM((GROUPS + 1, 2 * TILE, HEAD), jnp.bfloat16),
            pltpu.VMEM((2 * TILE, HEAD), jnp.bfloat16),
            pltpu.SemaphoreType.DMA((3,)),
            pltpu.SemaphoreType.DMA((3,)),
            pltpu.VMEM((GROUPS, 16, HEAD), jnp.bfloat16),
            pltpu.SemaphoreType.DMA((8,)),
            pltpu.SemaphoreType.DMA((8,)),
            pltpu.SemaphoreType.DMA,
        ],
        name="fetch_tiles",
        compiler_params=pltpu.CompilerParams(
            collective_id=0, has_side_effects=True, vmem_limit_bytes=16 << 20
        ),
    )(reads, prefix)


RING = (0, 3, 1, 2)


class Weights:
    def __init__(self, own, blocks, send, recv):
        self.own, self.blocks, self.send, self.recv = own, blocks, send, recv
        self.x, self.y, self.c, self.z = coords()
        self.started = []

    def at(self, f, s, other=False):
        c = 1 - self.c if other else self.c
        x = self.x + f * (1 - c) + s * c
        y = self.y + s * (1 - c) + f * c
        return place(x, y, c)

    def copy(self, kind, block, dp, rows=None, src=None):
        ref = self.blocks.at[block]
        if rows is not None:
            ref = ref.at[pl.ds(rows * 512, 512)]
        return remote(ref if src is None else src, ref, self.send.at[kind],
                      self.recv.at[kind], dp, self.z)

    def go(self, *args, **kw):
        copy = self.copy(*args, **kw)
        copy.start()
        self.started.append(copy)

    def to_sibling(self, jf, js, src=None):
        self.go(20 + 4 * jf + js, self.at(RING[jf], RING[js]),
                place(self.x, self.y, self.c + 1), src=src)

    def neighbours(self):
        return [self.at(1, 0), self.at(3, 0), self.at(0, 1), self.at(0, 3),
                place(self.x, self.y, self.c + 1)]

    def start(self):
        me = self.at(0, 0)
        self.go(0, me, self.at(1, 0), src=self.own)
        self.go(1, me, self.at(3, 0), src=self.own)
        self.go(4, me, self.at(0, 1), src=self.own)
        self.go(5, me, self.at(0, 3), src=self.own)
        self.to_sibling(0, 0, src=self.own)
        self.blocks[pl.ds(me, 1)] = self.own[...][None]

    def first_axis(self):
        me = self.at(0, 0)
        before, after = self.at(3, 0), self.at(1, 0)
        self.copy(0, before, me).wait_recv()
        self.go(2, before, after, rows=0)
        self.go(6, before, self.at(0, 1))
        self.go(7, before, self.at(0, 3))
        self.copy(1, after, me).wait_recv()
        self.go(3, after, before, rows=1)
        self.go(8, after, self.at(0, 1))
        self.go(9, after, self.at(0, 3))
        self.to_sibling(1, 0)
        self.to_sibling(2, 0)

    def opposite(self):
        me = self.at(0, 0)
        far = self.at(2, 0)
        self.copy(2, far, me, rows=0).wait_recv()
        self.copy(3, far, me, rows=1).wait_recv()
        self.go(10, far, self.at(0, 1))
        self.go(11, far, self.at(0, 3))
        self.to_sibling(3, 0)

    def second_axis(self, jf):
        me = self.at(0, 0)
        before, after = self.at(RING[jf], 3), self.at(RING[jf], 1)
        self.copy(4 + 2 * jf, before, me).wait_recv()
        self.go(12 + 2 * jf, before, self.at(0, 1), rows=0)
        self.copy(5 + 2 * jf, after, me).wait_recv()
        self.go(13 + 2 * jf, after, self.at(0, 3), rows=1)
        self.to_sibling(jf, 1)
        self.to_sibling(jf, 2)

    def last(self, jf):
        me = self.at(0, 0)
        far = self.at(RING[jf], 2)
        self.copy(12 + 2 * jf, far, me, rows=0).wait_recv()
        self.copy(13 + 2 * jf, far, me, rows=1).wait_recv()
        self.to_sibling(jf, 3)

    def finish(self):
        me = self.at(0, 0)
        for jf in range(4):
            for js in range(4):
                block = self.at(RING[jf], RING[js], other=True)
                self.copy(20 + 4 * jf + js, block, me).wait_recv()

    def drain(self):
        for copy in self.started:
            copy.wait_send()


def layer_kernel(visible, q, suffix, pre_k, pre_v, ids, w, out,
                 blocks, ka, va, qa, att, to_right, to_left, at_right, at_left,
                 w_send, w_recv, r_send, r_recv, l_send, l_recv):
    x, y, c, z = coords()
    me = lax.axis_index("dp")
    right, left = lax.rem(z + 1, NZ), lax.rem(z + NZ - 1, NZ)
    weights = Weights(w, blocks, w_send, w_recv)
    barrier = pltpu.get_barrier_semaphore()
    for peer in weights.neighbours():
        pl.semaphore_signal(barrier, inc=1, device_id=(peer, z), device_id_type=MESH)
    pl.semaphore_signal(barrier, inc=1, device_id=(me, right), device_id_type=MESH)
    pl.semaphore_signal(barrier, inc=1, device_id=(me, left), device_id_type=MESH)
    pl.semaphore_wait(barrier, 7)
    weights.start()

    ka[pl.ds(0, PRE), pl.ds(0, HEAD)] = pre_k[...]
    va[pl.ds(0, PRE), pl.ds(0, HEAD)] = pre_v[...]
    va[:, pl.ds(HEAD, HEAD)] = jnp.ones((KEYS, HEAD), jnp.bfloat16)
    row = lax.broadcasted_iota(jnp.int32, (BLK, BLK), 0)
    col = lax.broadcasted_iota(jnp.int32, (BLK, BLK), 1)
    qa[:, pl.ds(HEAD, HEAD)] = jnp.where(row == col, 1.0, 0.0).astype(jnp.bfloat16)

    def attend(b):
        token_ids = ids[:, pl.ds(b * BLK, BLK)]
        second = token_ids * 2 // 16 == 1
        for r in range(READS):
            zero = jnp.where(visible[0, 0, r] > 0, 0.0, BIG)
            one = jnp.where(visible[0, 1, r] > 0, 0.0, BIG)
            bias = jnp.where(second, one, zero)
            ka[pl.ds(r * TILE, TILE), pl.ds(HEAD, HEAD)] = jnp.broadcast_to(
                bias, (TILE, BLK)).astype(jnp.bfloat16)
        start = max(b - 1, 0) * BLK
        for part in range(2):
            base = start + part * BLK
            at = PRE + part * BLK
            key_ids = jnp.broadcast_to(
                ids[:, pl.ds(base, BLK)].astype(jnp.float32), (BLK, BLK)).T
            same = key_ids == token_ids.astype(jnp.float32)
            seen = same & (row + base <= col + b * BLK)
            ka[pl.ds(at, BLK), pl.ds(0, HEAD)] = suffix[pl.ds(base, BLK), pl.ds(0, HEAD)]
            ka[pl.ds(at, BLK), pl.ds(HEAD, HEAD)] = jnp.where(seen, 0.0, BIG).astype(jnp.bfloat16)
            va[pl.ds(at, BLK), pl.ds(0, HEAD)] = suffix[pl.ds(base, BLK), pl.ds(HEAD, HEAD)]

        def head(h, _):
            lanes = pl.ds(pl.multiple_of(h * HEAD, HEAD), HEAD)
            qa[:, pl.ds(0, HEAD)] = q[pl.ds(b * BLK, BLK), lanes]
            scores = lax.dot_general(qa[...], ka[...], (((1,), (1,)), ((), ())),
                                     preferred_element_type=jnp.float32)
            top = jnp.max(scores, axis=1, keepdims=True)
            probs = jnp.exp2((scores - top) * SCALE).astype(jnp.bfloat16)
            mixed = jnp.dot(probs, va[...], preferred_element_type=jnp.float32)
            att[pl.ds(b * BLK, BLK), lanes] = (
                mixed[:, :HEAD] / mixed[:, HEAD:]).astype(jnp.bfloat16)
            return 0

        lax.fori_loop(0, HEADS, head, 0)

    attend(0)
    weights.first_axis()
    attend(1)
    weights.opposite()
    weights.second_axis(0)
    attend(2)
    weights.second_axis(1)
    weights.second_axis(2)
    attend(3)
    weights.last(0)
    weights.second_axis(3)
    for jf in range(1, 4):
        weights.last(jf)
    weights.finish()

    def project(b, dest):
        base = lax.rem(dest, NZ) * 4
        wide = jnp.concatenate([blocks[base + i] for i in range(4)], axis=1)
        rows = pl.ds(pl.multiple_of(b * BLK, BLK), BLK)
        return jnp.dot(att[rows, :], wide, preferred_element_type=jnp.float32)

    half = COLS // 2

    def send(k, b, to, at, sems, peer):
        rows = pl.ds(pl.multiple_of(b * BLK, BLK), BLK)
        width = half if k == 4 else COLS
        return remote(to.at[k - 1, rows, pl.ds(0, width)], at.at[k - 1, rows, pl.ds(0, width)],
                      sems[0].at[k - 1, b], sems[1].at[k - 1, b], me, peer)

    def go_right(k, b):
        return send(k, b, to_right, at_right, (r_send, r_recv), right)

    def go_left(k, b):
        return send(k, b, to_left, at_left, (l_send, l_recv), left)

    def store(ref, k, b, value):
        rows = pl.ds(pl.multiple_of(b * BLK, BLK), BLK)
        ref[k - 1, rows, pl.ds(0, value.shape[1])] = value.astype(jnp.bfloat16)

    def arrived(ref, k, b):
        rows = pl.ds(pl.multiple_of(b * BLK, BLK), BLK)
        width = half if k == 3 else COLS
        return ref[k, rows, pl.ds(0, width)].astype(jnp.float32)

    def stage4(b, _):
        part = project(b, z + 4)
        store(to_right, 4, b, part[:, :half])
        go_right(4, b).start()
        store(to_left, 4, b, part[:, half:])
        go_left(4, b).start()
        return 0

    def stage3(b, _):
        part = project(b, z + 3)
        go_right(4, b).wait_recv()
        store(to_right, 3, b, jnp.concatenate(
            [part[:, :half] + arrived(at_right, 3, b), part[:, half:]], axis=1))
        go_right(3, b).start()
        part = project(b, z + 5)
        go_left(4, b).wait_recv()
        store(to_left, 3, b, jnp.concatenate(
            [part[:, :half], part[:, half:] + arrived(at_left, 3, b)], axis=1))
        go_left(3, b).start()
        return 0

    def stage(k):
        def body(b, _):
            part = project(b, z + k)
            go_right(k + 1, b).wait_recv()
            store(to_right, k, b, part + arrived(at_right, k, b))
            go_right(k, b).start()
            part = project(b, z + NZ - k)
            go_left(k + 1, b).wait_recv()
            store(to_left, k, b, part + arrived(at_left, k, b))
            go_left(k, b).start()
            return 0
        return body

    def final(b, _):
        part = project(b, z)
        go_right(1, b).wait_recv()
        part = part + arrived(at_right, 0, b)
        go_left(1, b).wait_recv()
        part = part + arrived(at_left, 0, b)
        rows = pl.ds(pl.multiple_of(b * BLK, BLK), BLK)
        out[rows, :] = part.astype(jnp.bfloat16)
        return 0

    for body in (stage4, stage3, stage(2), stage(1), final):
        lax.fori_loop(0, NBLK, body, 0)

    def drain(b, _):
        for k in range(1, 5):
            go_right(k, b).wait_send()
            go_left(k, b).wait_send()
        return 0

    lax.fori_loop(0, NBLK, drain, 0)
    weights.drain()


def layer(visible, q, suffix, pre_k, pre_v, ids, w):
    vmem = pl.BlockSpec(memory_space=pltpu.VMEM)
    bf16 = jnp.bfloat16
    return pl.pallas_call(
        layer_kernel,
        out_shape=jax.ShapeDtypeStruct((TOK, COLS), bf16),
        in_specs=[pl.BlockSpec(memory_space=pltpu.SMEM)] + [vmem] * 6,
        out_specs=vmem,
        scratch_shapes=[
            pltpu.VMEM((GROUPS, HEADS * HEAD, HEAD), bf16),
            pltpu.VMEM((KEYS, 2 * HEAD), bf16),
            pltpu.VMEM((KEYS, 2 * HEAD), bf16),
            pltpu.VMEM((BLK, 2 * HEAD), bf16),
            pltpu.VMEM((TOK, HEADS * HEAD), bf16),
            pltpu.VMEM((4, TOK, COLS), bf16),
            pltpu.VMEM((4, TOK, COLS), bf16),
            pltpu.VMEM((4, TOK, COLS), bf16),
            pltpu.VMEM((4, TOK, COLS), bf16),
            pltpu.SemaphoreType.DMA((36,)),
            pltpu.SemaphoreType.DMA((36,)),
            pltpu.SemaphoreType.DMA((4, NBLK)),
            pltpu.SemaphoreType.DMA((4, NBLK)),
            pltpu.SemaphoreType.DMA((4, NBLK)),
            pltpu.SemaphoreType.DMA((4, NBLK)),
        ],
        name="attend_project_reduce",
        compiler_params=pltpu.CompilerParams(
            collective_id=1, has_side_effects=True, vmem_limit_bytes=52 << 20
        ),
    )(visible, q, suffix, pre_k, pre_v, ids, w)


def local(queries, suffix_kv, prefix_key_value, answer_ids, read_tiles, visible, out_weight):
    pre_k, pre_v = fetch(read_tiles, prefix_key_value)
    return layer(visible, queries, suffix_kv, pre_k, pre_v, answer_ids, out_weight)


def solution(mesh):
    placed = (
        P("dp", "tensor"),
        P("dp", "tensor"),
        P("dp", None, "tensor"),
        P("dp", None),
        P("dp", None),
        P("dp", None, None),
        P("tensor", "dp"),
    )
    return jax.shard_map(
        local, mesh=mesh, in_specs=placed, out_specs=P("dp", "tensor"), check_vma=False
    )
```

time: 252 us -> 123 us (0.49)
  waiting for transfers between devices: 166 us -> 0 us
  Pallas kernels: 0 us -> 118 us
  matrix products: 33 us -> 0 us
  other arithmetic: 29.7 us -> 0 us
  between operations: 13.3 us -> 0.05 us
  local copies, waits for them, and re-layouts: 9.73 us -> 4.07 us
    pallas_call x0 -> x2, Pallas kernels: none -> 118 us  [the longest x1 90.2 us: layer(): pl.pallas_call(layer_kernel, out_shape=jax.ShapeDtypeStruct((TOK, COLS),...]
    reduce_scatter x1 -> x0, waiting for transfers between devices: 94.3 us -> none  [local(): lax.psum_scatter(partial_terms, 'tensor', scatter_dimension=1, tiled=True)]
    all_gather x2 -> x0, waiting for transfers between devices: 70.2 us -> none  [the longest x1 55.7 us: local(): column_block = lax.all_gather(prefix_key_value, 'dp', axis=0, tiled=True)]
    dot_general x17 -> x0, matrix products: 33 us -> none  [the longest x8 16.3 us: head_attention(): jnp.dot(head_query, head_keys.T, preferred_element_type=jnp.float32)]
    concatenate x2 -> x0, other arithmetic: 9.8 us -> none  [the longest x1 9.72 us: local(): jnp.concatenate([gathered_tiles.reshape(-1, row_width), suffix_kv], axis=0)]
    select_n x3 -> x0, other arithmetic: 8.82 us -> none  [the longest x1 8.13 us: local(): gathered_tiles = jnp.where(present[:, None, None], fetched, blank_tiles)]
    reduce_sum x8 -> x0, other arithmetic: 5.95 us -> none  [head_attention(): row_total = jnp.sum(exponent, axis=1, keepdims=True)]
    gather x2 -> x0, local copies, waits for them, and re-layouts: 4.18 us -> none  [local(): jnp.take(column_block, jnp.clip(my_reads, 0, column_block.shape[0] - 1),...]
  transfers between devices with their start and end apart: 3 -> 0, of which waited for: 3 -> 0; matrix products, arithmetic and copies ran while one was open for 24% -> 0% of each run, Pallas kernels for 0% -> 0%
where the time goes in v1:
time: 123 us; the launch traced here: 122 us
  Pallas kernels  118 us (96%)
  local copies, waits for them, and re-layouts  4.07 us (3%)
    pallas_call x1, Pallas kernels, layer(): pl.pallas_call(layer_kernel, out_shape=jax.ShapeDtypeStruct((TOK, COLS),...  90.2 us
    pallas_call x1, Pallas kernels, fetch(): pl.pallas_call(fetch_kernel, out_shape=(half, half), in_specs=[pl.BlockSp...  28 us
    unnamed x13, local copies, waits for them, and re-layouts  4.07 us

profile of v1, /device:TPU:1, one launch (start us, length us, event | category | flops | bytes accessed | tf_op | source)
XLA Modules:
  0.0 122.4 jit_solution(1074320310050128873)
XLA Ops:
  0.0 0.0 copy-start
  0.0 0.0 copy-start.2
  0.0 1.0 copy-done.2
  1.0 0.0 copy-start.5
  1.0 0.7 copy-done.5
  1.7 28.0 %fetch_tiles.1 = (bf16[1664,128]{1,0:T(8,128)(2,1)S(1)}, bf16[1664,128]{1,0:T(8,128)(2,1)S(1)}) custom-call(s32[1,26]{1,0:T(1,128)S(1)} %copy-done.5, bf16[8,64,256]{2,1,0:T(8,128)(2,1)S(1)} %copy-done.2), custom_call_target="tpu_custom_call" | custom-call | tf_op jit(solution)/shard_map/fetch_tiles/pallas_call | solution.py:129
  29.7 0.0 copy-start.3
  29.7 0.0 copy-start.4
  29.7 0.0 copy-done
  29.7 0.7 copy-done.3
  30.4 0.0 copy-done.4
  30.4 0.0 copy-start.1
  30.4 0.9 copy-done.1
  31.4 90.2 %attend_project_reduce.1 = bf16[512,512]{1,0:T(8,128)(2,1)S(1)} custom-call(s32[1,2,26]{2,1,0:T(2,128)S(1)} %copy-done.4, bf16[512,1024]{1,0:T(8,128)(2,1)} %q.1, bf16[512,256]{1,0:T(8,128)(2,1)S(1)} %copy-done, bf16[1664,128]{1,0:T(8,128)(2,1)S(1)} %get-tuple-element.7.pre_k, bf16[1664,128]{1,0:T(8,128)(2,1)S(1)} %get-tuple-element.8.pre_v, ...), custom_call_target="tpu_custom_call" | custom-call | tf_op jit(solution)/shard_map/attend_project_reduce/pallas_call | solution.py:412
  121.6 0.8 copy.9
Async XLA Ops:
  0.0 29.7 %copy-start = (bf16[512,256]{1,0:T(8,128)(2,1)S(1)}, bf16[512,256]{1,0:T(8,128)(2,1)}, u32[]{:S(2)}) copy-start(bf16[512,256]{1,0:T(8,128)(2,1)} %suffix.1) | copy-start | bytes 786436
  0.0 1.0 copy-start.2
  1.0 0.7 copy-start.5
  29.7 0.7 copy-start.3
  29.7 0.7 copy-start.4
  30.4 0.9 copy-start.1

commit v2 on v0

v2 whole, which is shorter than its diff:
```python
import functools

import jax
import jax.numpy as jnp
from jax import lax
from jax.experimental import pallas as pl
from jax.experimental.pallas import tpu as pltpu
from jax.sharding import PartitionSpec as P

HEAD = 128
TILE = 64
READS = 26
GROUPS = 32
TPS = 8
TOK = 512
HEADS = 8
BLK = 128
NBLK = TOK // BLK
PRE = READS * TILE
KEYS = PRE + 2 * BLK
NZ = 8
COLS = 512
MESH = pl.DeviceIdType.MESH
PAIR = 2 * BLK
BF16 = jnp.bfloat16
F32 = jnp.float32
BIG = -1e30
LOG2E = 1.4426950408889634
SCALE = HEAD ** (-0.5) * LOG2E


def coords():
    g = lax.axis_index("dp")
    return g // 8, lax.rem(g // 2, 4), lax.rem(g, 2), lax.axis_index("tensor")


def place(x, y, c):
    return lax.rem(x, 4) * 8 + lax.rem(y, 4) * 2 + lax.rem(c, 2)


def remote(src, dst, send, recv, dp, tensor):
    return pltpu.make_async_remote_copy(
        src_ref=src, dst_ref=dst, send_sem=send, recv_sem=recv,
        device_id=(dp, tensor), device_id_type=MESH,
    )


class Tiles:
    def __init__(self, reads, prefix, ask, table, asked, packed, got, hot_out, hot_recv,
                 sem_send, sem_recv, spread_send, spread_recv, local_sem):
        self.reads, self.prefix, self.ask, self.table, self.asked = reads, prefix, ask, table, asked
        self.packed, self.got, self.hot_out, self.hot_recv = packed, got, hot_out, hot_recv
        self.sem_send, self.sem_recv, self.local_sem = sem_send, sem_recv, local_sem
        self.spread_send, self.spread_recv = spread_send, spread_recv
        self.x, self.y, self.c, self.z = coords()
        self.me = lax.axis_index("dp")
        self.peers = [place(self.x + k // 8, self.y + (k // 2) % 4, self.c + k % 2)
                      for k in range(1, GROUPS)]

    def plan(self):
        lane = lax.broadcasted_iota(jnp.int32, (1, 128), 1)
        first = jnp.full((1, 128), TPS, jnp.int32)
        last = jnp.full((1, 128), -1, jnp.int32)
        self.tiles = [self.reads[0, r] for r in range(READS)]
        for tile in self.tiles:
            here = lane == tile // TPS
            first = jnp.where(here, jnp.minimum(first, tile % TPS), first)
            last = jnp.where(here, jnp.maximum(last, tile % TPS), last)
        twice = last > first
        self.hot_owner = jnp.max(jnp.where(twice, lane, 0))
        self.hot_second = jnp.max(jnp.where(twice, last, 0))
        mine = jnp.where(first == TPS, 0, first)
        self.ask[...] = mine
        self.table[pl.ds(self.me, 1)] = mine[None]

    def cut(self):
        second = self.prefix[self.hot_second]
        self.hot_out[pl.ds(0, TILE)] = second[:, :HEAD]
        self.hot_out[pl.ds(TILE, TILE)] = second[:, HEAD:]
        self.part = pl.multiple_of(lax.rem(self.me, 8) * 16, 16)
        self.hot_recv[pl.ds(self.me, 1)] = self.hot_out[pl.ds(self.part, 16)][None]

    def request(self):
        for peer in self.peers:
            remote(self.ask, self.table.at[self.me], self.sem_send.at[0], self.sem_recv.at[0],
                   peer, self.z).start()

    def pieces(self):
        for peer in self.peers:
            part = pl.multiple_of(lax.rem(peer, 8) * 16, 16)
            remote(self.hot_out.at[pl.ds(part, 16)], self.hot_recv.at[self.me],
                   self.sem_send.at[1], self.sem_recv.at[1], peer, self.z).start()

    def wait_all(self, ref, sem):
        part = ref.at[pl.ds(0, GROUPS - 1)]
        pltpu.make_async_copy(part, part, sem).wait()

    def answer(self):
        me, z = self.me, self.z
        self.wait_all(self.table, self.sem_recv.at[0])
        load = pltpu.make_async_copy(self.table, self.asked, self.local_sem)
        load.start()
        load.wait()
        for k, peer in enumerate(self.peers):
            tile = self.prefix[self.asked[peer, 0, me]]
            self.packed[k, pl.ds(0, TILE)] = tile[:, :HEAD]
            self.packed[k, pl.ds(TILE, TILE)] = tile[:, HEAD:]
            remote(self.packed.at[k], self.got.at[me], self.sem_send.at[2],
                   self.sem_recv.at[2], peer, z).start()
        own = self.prefix[self.asked[me, 0, me]]
        self.got[pl.ds(me, 1), pl.ds(0, TILE)] = own[:, :HEAD][None]
        self.got[pl.ds(me, 1), pl.ds(TILE, TILE)] = own[:, HEAD:][None]

    def spread(self):
        self.wait_all(self.hot_recv, self.sem_recv.at[1])
        ref = self.got.at[GROUPS, pl.ds(self.part, 16)]
        self.got[GROUPS, pl.ds(self.part, 16)] = self.hot_recv[self.hot_owner]
        self.spreads = []
        for k in range(1, 8):
            copy = remote(ref, ref, self.spread_send.at[k], self.spread_recv.at[k],
                          place(self.x, self.y + k // 2, self.c + k % 2), self.z)
            copy.start()
            self.spreads.append(copy)

    def receive(self):
        self.wait_all(self.got, self.sem_recv.at[2])
        for copy in self.spreads:
            copy.wait_recv()

    def tile(self, r):
        owner = self.tiles[r] // TPS
        second = (owner == self.hot_owner) & (self.tiles[r] % TPS == self.hot_second)
        return self.got[jnp.where(second, GROUPS, owner)]

    def drain(self):
        self.wait_all(self.table, self.sem_send.at[0])
        self.wait_all(self.hot_recv, self.sem_send.at[1])
        self.wait_all(self.packed, self.sem_send.at[2])
        for copy in self.spreads:
            copy.wait_send()


RING = (0, 3, 1, 2)


class Weights:
    def __init__(self, blocks, send, recv):
        self.blocks, self.send, self.recv = blocks, send, recv
        self.x, self.y, self.c, self.z = coords()
        self.started = []

    def at(self, f, s, other=False):
        c = 1 - self.c if other else self.c
        x = self.x + f * (1 - c) + s * c
        y = self.y + s * (1 - c) + f * c
        return place(x, y, c)

    def copy(self, kind, block, dp, rows=None):
        ref = self.blocks.at[block]
        if rows is not None:
            ref = ref.at[pl.ds(rows * 512, 512)]
        return remote(ref, ref, self.send.at[kind], self.recv.at[kind], dp, self.z)

    def go(self, *args, **kw):
        copy = self.copy(*args, **kw)
        copy.start()
        self.started.append(copy)

    def to_sibling(self, jf, js):
        self.go(20 + 4 * jf + js, self.at(RING[jf], RING[js]),
                place(self.x, self.y, self.c + 1))

    def start(self):
        me = self.at(0, 0)
        self.go(0, me, self.at(1, 0))
        self.go(1, me, self.at(3, 0))
        self.go(4, me, self.at(0, 1))
        self.go(5, me, self.at(0, 3))
        self.to_sibling(0, 0)

    def first_axis(self):
        me = self.at(0, 0)
        before, after = self.at(3, 0), self.at(1, 0)
        self.copy(0, before, me).wait_recv()
        self.go(2, before, after, rows=0)
        self.go(6, before, self.at(0, 1))
        self.go(7, before, self.at(0, 3))
        self.copy(1, after, me).wait_recv()
        self.go(3, after, before, rows=1)
        self.go(8, after, self.at(0, 1))
        self.go(9, after, self.at(0, 3))
        self.to_sibling(1, 0)
        self.to_sibling(2, 0)

    def opposite(self):
        me = self.at(0, 0)
        far = self.at(2, 0)
        self.copy(2, far, me, rows=0).wait_recv()
        self.copy(3, far, me, rows=1).wait_recv()
        self.go(10, far, self.at(0, 1))
        self.go(11, far, self.at(0, 3))
        self.to_sibling(3, 0)

    def second_axis(self, jf):
        me = self.at(0, 0)
        before, after = self.at(RING[jf], 3), self.at(RING[jf], 1)
        self.copy(4 + 2 * jf, before, me).wait_recv()
        self.go(12 + 2 * jf, before, self.at(0, 1), rows=0)
        self.copy(5 + 2 * jf, after, me).wait_recv()
        self.go(13 + 2 * jf, after, self.at(0, 3), rows=1)
        self.to_sibling(jf, 1)
        self.to_sibling(jf, 2)

    def last(self, jf):
        me = self.at(0, 0)
        far = self.at(RING[jf], 2)
        self.copy(12 + 2 * jf, far, me, rows=0).wait_recv()
        self.copy(13 + 2 * jf, far, me, rows=1).wait_recv()
        self.to_sibling(jf, 3)

    def finish(self):
        me = self.at(0, 0)
        for jf in range(4):
            for js in range(4):
                block = self.at(RING[jf], RING[js], other=True)
                self.copy(20 + 4 * jf + js, block, me).wait_recv()

    def drain(self):
        for copy in self.started:
            copy.wait_send()


class Reduce:
    def __init__(self, att, blocks, out, to_right, to_left, at_right, at_left,
                 r_send, r_recv, l_send, l_recv):
        self.att, self.blocks, self.out = att, blocks, out
        self.me, self.z = lax.axis_index("dp"), lax.axis_index("tensor")
        right, left = lax.rem(self.z + 1, NZ), lax.rem(self.z + NZ - 1, NZ)
        self.right = (to_right, at_right, r_send, r_recv, right)
        self.left = (to_left, at_left, l_send, l_recv, left)

    def rows(self, b):
        return pl.ds(pl.multiple_of(b * BLK, BLK), BLK)

    def project(self, b, hops):
        base = lax.rem(self.z + NZ + hops, NZ) * 4
        wide = jnp.concatenate([self.blocks[base + i] for i in range(4)], axis=1)
        return jnp.dot(self.att[self.rows(b), :], wide, preferred_element_type=F32)

    def copy(self, way, k, b):
        to, at, send, recv, peer = way
        part = (k - 1, self.rows(b), pl.ds(0, COLS // 2 if k == 4 else COLS))
        return remote(to.at[part], at.at[part], send.at[k - 1, b], recv.at[k - 1, b],
                      self.me, peer)

    def send(self, way, k, b, value):
        way[0][k - 1, self.rows(b), pl.ds(0, value.shape[1])] = value.astype(BF16)
        self.copy(way, k, b).start()

    def arrived(self, way, k, b):
        self.copy(way, k + 1, b).wait_recv()
        return way[1][k, self.rows(b), pl.ds(0, COLS // 2 if k == 3 else COLS)].astype(F32)

    def stage(self, k):
        half = COLS // 2

        def body(b, _):
            if k == 4:
                part = self.project(b, 4)
                self.send(self.right, 4, b, part[:, :half])
                self.send(self.left, 4, b, part[:, half:])
            elif k == 0:
                part = self.project(b, 0)
                part = part + self.arrived(self.right, 0, b)
                part = part + self.arrived(self.left, 0, b)
                self.out[self.rows(b), :] = part.astype(BF16)
            else:
                for way, hops in ((self.right, k), (self.left, -k)):
                    part = self.project(b, hops)
                    come = self.arrived(way, k, b)
                    if k == 3 and hops > 0:
                        part = jnp.concatenate([part[:, :half] + come, part[:, half:]], axis=1)
                    elif k == 3:
                        part = jnp.concatenate([part[:, :half], part[:, half:] + come], axis=1)
                    else:
                        part = part + come
                    self.send(way, k, b, part)
            return 0

        lax.fori_loop(0, NBLK, body, 0)

    def drain(self):
        def body(b, _):
            for k in range(1, 5):
                self.copy(self.right, k, b).wait_send()
                self.copy(self.left, k, b).wait_send()
            return 0

        lax.fori_loop(0, NBLK, body, 0)


class Attention:
    def __init__(self, visible, ids, q, suffix, ka, va, qa, scores, att):
        self.visible, self.ids, self.q, self.suffix = visible, ids, q, suffix
        self.ka, self.va, self.qa, self.scores, self.att = ka, va, qa, scores, att

    def fixed(self):
        row = lax.broadcasted_iota(jnp.int32, (BLK, BLK), 0)
        col = lax.broadcasted_iota(jnp.int32, (BLK, BLK), 1)
        self.row, self.col = row, col
        eye = jnp.where(row == col, 1.0, 0.0).astype(BF16)
        for slot in range(2):
            for j in range(2):
                self.qa[slot, pl.ds(j * BLK, BLK), pl.ds(HEAD, HEAD)] = eye
            self.va[slot, :, pl.ds(HEAD, HEAD)] = jnp.ones((KEYS, HEAD), BF16)
        self.down = [jnp.broadcast_to(self.ids[:, pl.ds(b * BLK, BLK)].astype(F32), (BLK, BLK)).T
                     for b in range(NBLK)]

    def bias(self, b):
        slot = b % 2
        second = self.down[b] >= 8.0
        for r in range(0, READS, 2):
            lines = [jnp.where(self.col < TILE,
                               jnp.where(self.visible[0, n, r] > 0, 0.0, BIG),
                               jnp.where(self.visible[0, n, r + 1] > 0, 0.0, BIG))
                     for n in range(2)]
            self.ka[slot, pl.ds(HEAD, HEAD), pl.ds(r * TILE, BLK)] = jnp.where(
                second, lines[1], lines[0]).astype(BF16)
        start = max(b - 1, 0) * BLK
        for part in range(2):
            base = start + part * BLK
            at = pl.ds(PRE + part * BLK, BLK)
            same = self.down[b] == self.ids[:, pl.ds(base, BLK)].astype(F32)
            seen = same & (self.col + base <= self.row + b * BLK)
            self.ka[slot, pl.ds(HEAD, HEAD), at] = jnp.where(seen, 0.0, BIG).astype(BF16)
            self.ka[slot, pl.ds(0, HEAD), at] = self.suffix[pl.ds(base, BLK), pl.ds(0, HEAD)].T
            self.va[slot, at, pl.ds(0, HEAD)] = self.suffix[pl.ds(base, BLK), pl.ds(HEAD, HEAD)]

    def take(self, tiles):
        for r in range(0, READS, 2):
            one, two = tiles.tile(r), tiles.tile(r + 1)
            across = jnp.concatenate([one[:TILE], two[:TILE]], axis=0).T
            for slot in range(2):
                self.ka[slot, pl.ds(0, HEAD), pl.ds(r * TILE, BLK)] = across
                self.va[slot, pl.ds(r * TILE, TILE), pl.ds(0, HEAD)] = one[TILE:]
                self.va[slot, pl.ds((r + 1) * TILE, TILE), pl.ds(0, HEAD)] = two[TILE:]

    def score(self, i):
        b, h = i // 4, i % 4 * 2
        for j in range(2):
            self.qa[i % 2, pl.ds(j * BLK, BLK), pl.ds(0, HEAD)] = (
                self.q[pl.ds(b * BLK, BLK), pl.ds((h + j) * HEAD, HEAD)])
        self.scores[i % 2] = jnp.dot(self.qa[i % 2], self.ka[b % 2], preferred_element_type=F32)

    def rest(self, i):
        b, h = i // 4, i % 4 * 2
        scores = self.scores[i % 2]
        top = jnp.max(scores, axis=1, keepdims=True)
        probs = jnp.exp2((scores - top) * SCALE).astype(BF16)
        mixed = jnp.dot(probs, self.va[b % 2], preferred_element_type=F32)
        done = (mixed[:, :HEAD] / mixed[:, HEAD:]).astype(BF16)
        for j in range(2):
            self.att[pl.ds(b * BLK, BLK), pl.ds((h + j) * HEAD, HEAD)] = done[j * BLK:(j + 1) * BLK]

    def block(self, b):
        for i in range(4 * b, 4 * b + 4):
            if i % 4 == 3 and b + 1 < NBLK:
                self.bias(b + 1)
            if i + 1 < 4 * NBLK:
                self.score(i + 1)
            self.rest(i)


def layer_kernel(reads, visible, prefix_hbm, q_hbm, suffix_hbm, ids, w_hbm, out,
                 prefix, q, suffix, load_sem, blocks, w_send, w_recv,
                 ask, table, asked, packed, got, hot_out, hot_recv,
                 t_send, t_recv, spread_send, spread_recv, local_sem,
                 ka, va, qa, scores, att,
                 to_right, to_left, at_right, at_left, r_send, r_recv, l_send, l_recv):
    me, z = lax.axis_index("dp"), lax.axis_index("tensor")
    loads = [pltpu.make_async_copy(src, dst, load_sem.at[i]) for i, (src, dst) in enumerate(
        ((prefix_hbm, prefix), (w_hbm, blocks.at[me]), (suffix_hbm, suffix), (q_hbm, q)))]
    for load in loads:
        load.start()
    tiles = Tiles(reads, prefix, ask, table, asked, packed, got, hot_out, hot_recv,
                  t_send, t_recv, spread_send, spread_recv, local_sem)
    weights = Weights(blocks, w_send, w_recv)
    reduce = Reduce(att, blocks, out, to_right, to_left, at_right, at_left,
                    r_send, r_recv, l_send, l_recv)
    attention = Attention(visible, ids, q, suffix, ka, va, qa, scores, att)

    barrier = pltpu.get_barrier_semaphore()
    for peer in tiles.peers:
        pl.semaphore_signal(barrier, inc=1, device_id=(peer, z), device_id_type=MESH)
    for way in (reduce.right, reduce.left):
        pl.semaphore_signal(barrier, inc=1, device_id=(me, way[4]), device_id_type=MESH)
    tiles.plan()
    loads[0].wait()
    tiles.cut()
    loads[1].wait()
    pl.semaphore_wait(barrier, GROUPS + 1)

    tiles.request()
    tiles.pieces()
    attention.fixed()
    tiles.answer()
    weights.start()
    tiles.spread()
    loads[2].wait()
    loads[3].wait()
    attention.bias(0)
    tiles.receive()
    attention.take(tiles)
    attention.score(0)
    weights.first_axis()
    attention.block(0)
    weights.opposite()
    weights.second_axis(0)
    attention.block(1)
    weights.second_axis(1)
    weights.second_axis(2)
    attention.block(2)
    weights.last(0)
    weights.second_axis(3)
    attention.block(3)
    for jf in range(1, 4):
        weights.last(jf)
    weights.finish()
    for k in (4, 3, 2, 1, 0):
        reduce.stage(k)
    reduce.drain()
    weights.drain()
    tiles.drain()


def layer(reads, visible, prefix, q, suffix, ids, w):
    smem = pl.BlockSpec(memory_space=pltpu.SMEM)
    vmem = pl.BlockSpec(memory_space=pltpu.VMEM)
    hbm = pl.BlockSpec(memory_space=pl.ANY)
    dma = pltpu.SemaphoreType.DMA
    return pl.pallas_call(
        layer_kernel,
        out_shape=jax.ShapeDtypeStruct((TOK, COLS), BF16),
        in_specs=[smem, smem, hbm, hbm, hbm, vmem, hbm],
        out_specs=vmem,
        scratch_shapes=[
            pltpu.VMEM((TPS, TILE, 2 * HEAD), BF16),
            pltpu.VMEM((TOK, HEADS * HEAD), BF16),
            pltpu.VMEM((TOK, 2 * HEAD), BF16),
            dma((4,)),
            pltpu.VMEM((GROUPS, HEADS * HEAD, HEAD), BF16),
            dma((36,)),
            dma((36,)),
            pltpu.VMEM((1, 128), jnp.int32),
            pltpu.VMEM((GROUPS, 1, 128), jnp.int32),
            pltpu.SMEM((GROUPS, 1, 128), jnp.int32),
            pltpu.VMEM((GROUPS - 1, 2 * TILE, HEAD), BF16),
            pltpu.VMEM((GROUPS + 1, 2 * TILE, HEAD), BF16),
            pltpu.VMEM((2 * TILE, HEAD), BF16),
            pltpu.VMEM((GROUPS, 16, HEAD), BF16),
            dma((3,)),
            dma((3,)),
            dma((8,)),
            dma((8,)),
            dma,
            pltpu.VMEM((2, 2 * HEAD, KEYS), BF16),
            pltpu.VMEM((2, KEYS, 2 * HEAD), BF16),
            pltpu.VMEM((2, PAIR, 2 * HEAD), BF16),
            pltpu.VMEM((2, PAIR, KEYS), F32),
            pltpu.VMEM((TOK, HEADS * HEAD), BF16),
            pltpu.VMEM((4, TOK, COLS), BF16),
            pltpu.VMEM((4, TOK, COLS), BF16),
            pltpu.VMEM((4, TOK, COLS), BF16),
            pltpu.VMEM((4, TOK, COLS), BF16),
            dma((4, NBLK)),
            dma((4, NBLK)),
            dma((4, NBLK)),
            dma((4, NBLK)),
        ],
        name="fetch_attend_project_reduce",
        compiler_params=pltpu.CompilerParams(
            collective_id=0, has_side_effects=True, vmem_limit_bytes=52 << 20
        ),
    )(reads, visible, prefix, q, suffix, ids, w)


def local(queries, suffix_kv, prefix_key_value, answer_ids, read_tiles, visible, out_weight):
    return layer(read_tiles, visible, prefix_key_value, queries, suffix_kv, answer_ids,
                 out_weight)


def solution(mesh):
    placed = (
        P("dp", "tensor"),
        P("dp", "tensor"),
        P("dp", None, "tensor"),
        P("dp", None),
        P("dp", None),
        P("dp", None, None),
        P("tensor", "dp"),
    )
    return jax.shard_map(
        local, mesh=mesh, in_specs=placed, out_specs=P("dp", "tensor"), check_vma=False
    )
```

time: 252 us -> 107 us (0.42)
  waiting for transfers between devices: 166 us -> 0 us
  Pallas kernels: 0 us -> 101 us
  matrix products: 33 us -> 0 us
  other arithmetic: 29.7 us -> 0 us
  between operations: 13.3 us -> 0.02 us
  local copies, waits for them, and re-layouts: 9.73 us -> 5.66 us
    pallas_call x0 -> x1, Pallas kernels: none -> 101 us  [layer(): pl.pallas_call(layer_kernel, out_shape=jax.ShapeDtypeStruct((TOK, COLS),...]
    reduce_scatter x1 -> x0, waiting for transfers between devices: 94.3 us -> none  [local(): lax.psum_scatter(partial_terms, 'tensor', scatter_dimension=1, tiled=True)]
    all_gather x2 -> x0, waiting for transfers between devices: 70.2 us -> none  [the longest x1 55.7 us: local(): column_block = lax.all_gather(prefix_key_value, 'dp', axis=0, tiled=True)]
    dot_general x17 -> x0, matrix products: 33 us -> none  [the longest x8 16.3 us: head_attention(): jnp.dot(head_query, head_keys.T, preferred_element_type=jnp.float32)]
    concatenate x2 -> x0, other arithmetic: 9.8 us -> none  [the longest x1 9.72 us: local(): jnp.concatenate([gathered_tiles.reshape(-1, row_width), suffix_kv], axis=0)]
    select_n x3 -> x0, other arithmetic: 8.82 us -> none  [the longest x1 8.13 us: local(): gathered_tiles = jnp.where(present[:, None, None], fetched, blank_tiles)]
    reduce_sum x8 -> x0, other arithmetic: 5.95 us -> none  [head_attention(): row_total = jnp.sum(exponent, axis=1, keepdims=True)]
    gather x2 -> x0, local copies, waits for them, and re-layouts: 4.18 us -> none  [local(): jnp.take(column_block, jnp.clip(my_reads, 0, column_block.shape[0] - 1),...]
  transfers between devices with their start and end apart: 3 -> 0, of which waited for: 3 -> 0; matrix products, arithmetic and copies ran while one was open for 24% -> 0% of each run, Pallas kernels for 0% -> 0%
where the time goes in v2:
time: 107 us
  Pallas kernels  101 us (94%)
  local copies, waits for them, and re-layouts  5.66 us (5%)
    pallas_call x1, Pallas kernels, layer(): pl.pallas_call(layer_kernel, out_shape=jax.ShapeDtypeStruct((TOK, COLS),...  101 us
    unnamed x13, local copies, waits for them, and re-layouts  5.66 us

profile of v2, /device:TPU:1, one launch (start us, length us, event | category | flops | bytes accessed | tf_op | source)
XLA Modules:
  0.0 106.6 jit_solution(5887934183588001130)
XLA Ops:
  0.0 0.0 copy-start
  0.0 0.9 copy-done
  1.0 0.0 copy-start.1
  1.0 0.9 copy-done.1
  1.9 0.0 copy-start.2
  1.9 0.9 copy-done.2
  2.9 0.0 copy-start.3
  2.9 0.7 copy-done.3
  3.5 0.0 copy-start.4
  3.5 0.7 copy-done.4
  4.2 0.0 copy-start.5
  4.2 0.7 copy-done.5
  4.9 100.9 %fetch_attend_project_reduce.1 = bf16[512,512]{1,0:T(8,128)(2,1)S(1)} custom-call(s32[1,26]{1,0:T(1,128)S(1)} %copy-done.5, s32[1,2,26]{2,1,0:T(2,128)S(1)} %copy-done.4, bf16[8,64,256]{2,1,0:T(8,128)(2,1)S(1)} %copy-done, bf16[512,1024]{1,0:T(8,128)(2,1)} %q_hbm.1, bf16[512,256]{1,0:T(8,128)(2,1)S(1)} %copy-done.1, s32[1,512]{1,0:T(1,128)S(1)} %copy-done.3, ...), custom_call_target="tpu_custom_call" | custom-call | tf_op jit(solution)/shard_map/fetch_attend_project_reduce/pallas_call | solution.py:441
  105.8 0.8 copy.9
Async XLA Ops:
  0.0 0.9 copy-start
  1.0 0.9 copy-start.1
  1.9 0.9 copy-start.2
  2.9 0.7 copy-start.3
  3.5 0.7 copy-start.4
  4.2 0.7 copy-start.5

commit v3 on v2

--- a/solution.py
+++ b/solution.py
@@ -20,6 +20,7 @@
 KEYS = PRE + 2 * BLK
 NZ = 8
 COLS = 512
+VMEM = 63 << 20
 MESH = pl.DeviceIdType.MESH
 PAIR = 2 * BLK
 BF16 = jnp.bfloat16
@@ -140,20 +141,26 @@
             copy.wait_send()
 
 
-RING = (0, 3, 1, 2)
-
-
 class Weights:
     def __init__(self, blocks, send, recv):
         self.blocks, self.send, self.recv = blocks, send, recv
         self.x, self.y, self.c, self.z = coords()
-        self.started = []
-
-    def at(self, f, s, other=False):
-        c = 1 - self.c if other else self.c
-        x = self.x + f * (1 - c) + s * c
-        y = self.y + s * (1 - c) + f * c
-        return place(x, y, c)
+        c = self.c
+        x_mate, y_mate = 1 + 2 * lax.rem(self.x, 2), 1 + 2 * lax.rem(self.y, 2)
+        first = x_mate * (1 - c) + y_mate * c
+        second = y_mate * (1 - c) + x_mate * c
+        self.f, self.s = (0, first, 4 - first, 2), (0, second, 4 - second, 2)
+        self.sibling = place(self.x, self.y, c + 1)
+
+    def at(self, jf, js):
+        c = self.c
+        f, s = self.f[jf], self.s[js]
+        return place(self.x + f * (1 - c) + s * c, self.y + s * (1 - c) + f * c, c)
+
+    def other_core(self, jf, js):
+        c = 1 - self.c
+        f, s = self.s[jf], self.f[js]
+        return place(self.x + f * (1 - c) + s * c, self.y + s * (1 - c) + f * c, c)
 
     def copy(self, kind, block, dp, rows=None):
         ref = self.blocks.at[block]
@@ -161,73 +168,65 @@
             ref = ref.at[pl.ds(rows * 512, 512)]
         return remote(ref, ref, self.send.at[kind], self.recv.at[kind], dp, self.z)
 
-    def go(self, *args, **kw):
-        copy = self.copy(*args, **kw)
-        copy.start()
-        self.started.append(copy)
-
-    def to_sibling(self, jf, js):
-        self.go(20 + 4 * jf + js, self.at(RING[jf], RING[js]),
-                place(self.x, self.y, self.c + 1))
+    def sent(self, kind):
+        if kind < 2:
+            return self.copy(kind, self.at(0, 0), self.at(kind + 1, 0))
+        if kind < 4:
+            return self.copy(kind, self.at(kind - 1, 0), self.at(4 - kind, 0), rows=kind - 2)
+        if kind < 12:
+            j, way = (kind - 4) // 2, kind % 2
+            return self.copy(kind, self.at(j, 0), self.at(0, 1 + way))
+        if kind < 20:
+            j, way = (kind - 12) // 2, kind % 2
+            return self.copy(kind, self.at(j, 1 + way), self.at(0, 2 - way), rows=way)
+        return self.copy(kind, self.at((kind - 20) // 4, kind % 4), self.sibling)
+
+    def go(self, *kinds):
+        for kind in kinds:
+            self.sent(kind).start()
+
+    def come(self, *kinds):
+        me = self.at(0, 0)
+        for kind in kinds:
+            if kind < 2:
+                copy = self.copy(kind, self.at(kind + 1, 0), me)
+            elif kind < 4:
+                copy = self.copy(kind, self.at(3, 0), me, rows=kind - 2)
+            elif kind < 12:
+                copy = self.copy(kind, self.at((kind - 4) // 2, 1 + kind % 2), me)
+            elif kind < 20:
+                copy = self.copy(kind, self.at((kind - 12) // 2, 3), me, rows=kind % 2)
+            else:
+                copy = self.copy(kind, self.other_core((kind - 20) // 4, kind % 4), me)
+            copy.wait_recv()
 
     def start(self):
-        me = self.at(0, 0)
-        self.go(0, me, self.at(1, 0))
-        self.go(1, me, self.at(3, 0))
-        self.go(4, me, self.at(0, 1))
-        self.go(5, me, self.at(0, 3))
-        self.to_sibling(0, 0)
-
-    def first_axis(self):
-        me = self.at(0, 0)
-        before, after = self.at(3, 0), self.at(1, 0)
-        self.copy(0, before, me).wait_recv()
-        self.go(2, before, after, rows=0)
-        self.go(6, before, self.at(0, 1))
-        self.go(7, before, self.at(0, 3))
-        self.copy(1, after, me).wait_recv()
-        self.go(3, after, before, rows=1)
-        self.go(8, after, self.at(0, 1))
-        self.go(9, after, self.at(0, 3))
-        self.to_sibling(1, 0)
-        self.to_sibling(2, 0)
+        self.go(0, 1, 4, 5, 20)
+
+    def ring(self):
+        self.come(0)
+        self.go(2, 6, 7, 24)
+        self.come(1)
+        self.go(3, 8, 9, 28)
 
     def opposite(self):
-        me = self.at(0, 0)
-        far = self.at(2, 0)
-        self.copy(2, far, me, rows=0).wait_recv()
-        self.copy(3, far, me, rows=1).wait_recv()
-        self.go(10, far, self.at(0, 1))
-        self.go(11, far, self.at(0, 3))
-        self.to_sibling(3, 0)
-
-    def second_axis(self, jf):
-        me = self.at(0, 0)
-        before, after = self.at(RING[jf], 3), self.at(RING[jf], 1)
-        self.copy(4 + 2 * jf, before, me).wait_recv()
-        self.go(12 + 2 * jf, before, self.at(0, 1), rows=0)
-        self.copy(5 + 2 * jf, after, me).wait_recv()
-        self.go(13 + 2 * jf, after, self.at(0, 3), rows=1)
-        self.to_sibling(jf, 1)
-        self.to_sibling(jf, 2)
-
-    def last(self, jf):
-        me = self.at(0, 0)
-        far = self.at(RING[jf], 2)
-        self.copy(12 + 2 * jf, far, me, rows=0).wait_recv()
-        self.copy(13 + 2 * jf, far, me, rows=1).wait_recv()
-        self.to_sibling(jf, 3)
+        self.come(2, 3)
+        self.go(10, 11, 32)
+
+    def across(self, j):
+        self.come(4 + 2 * j, 5 + 2 * j)
+        self.go(12 + 2 * j, 13 + 2 * j, 21 + 4 * j, 22 + 4 * j)
+
+    def last(self, j):
+        self.come(12 + 2 * j, 13 + 2 * j)
+        self.go(23 + 4 * j)
 
     def finish(self):
-        me = self.at(0, 0)
-        for jf in range(4):
-            for js in range(4):
-                block = self.at(RING[jf], RING[js], other=True)
-                self.copy(20 + 4 * jf + js, block, me).wait_recv()
+        self.come(*range(20, 36))
 
     def drain(self):
-        for copy in self.started:
-            copy.wait_send()
+        for kind in range(36):
+            self.sent(kind).wait_send()
 
 
 class Reduce:
@@ -362,13 +361,12 @@
         for j in range(2):
             self.att[pl.ds(b * BLK, BLK), pl.ds((h + j) * HEAD, HEAD)] = done[j * BLK:(j + 1) * BLK]
 
-    def block(self, b):
-        for i in range(4 * b, 4 * b + 4):
-            if i % 4 == 3 and b + 1 < NBLK:
-                self.bias(b + 1)
-            if i + 1 < 4 * NBLK:
-                self.score(i + 1)
-            self.rest(i)
+    def pair(self, i):
+        if i % 4 == 3 and i + 1 < 4 * NBLK:
+            self.bias(i // 4 + 1)
+        if i + 1 < 4 * NBLK:
+            self.score(i + 1)
+        self.rest(i)
 
 
 def layer_kernel(reads, visible, prefix_hbm, q_hbm, suffix_hbm, ids, w_hbm, out,
@@ -401,30 +399,29 @@
     pl.semaphore_wait(barrier, GROUPS + 1)
 
     tiles.request()
+    weights.start()
     tiles.pieces()
     attention.fixed()
     tiles.answer()
-    weights.start()
+    weights.ring()
     tiles.spread()
     loads[2].wait()
     loads[3].wait()
     attention.bias(0)
+    weights.opposite()
+    weights.across(0)
     tiles.receive()
     attention.take(tiles)
     attention.score(0)
-    weights.first_axis()
-    attention.block(0)
-    weights.opposite()
-    weights.second_axis(0)
-    attention.block(1)
-    weights.second_axis(1)
-    weights.second_axis(2)
-    attention.block(2)
-    weights.last(0)
-    weights.second_axis(3)
-    attention.block(3)
-    for jf in range(1, 4):
-        weights.last(jf)
+    beside = {
+        0: [(weights.across, 1)], 2: [(weights.across, 2)], 4: [(weights.across, 3)],
+        6: [(weights.last, 0)], 8: [(weights.last, 1)], 10: [(weights.last, 2)],
+        12: [(weights.last, 3)],
+    }
+    for i in range(4 * NBLK):
+        attention.pair(i)
+        for step, *j in beside.get(i, ()):
+            step(*j)
     weights.finish()
     for k in (4, 3, 2, 1, 0):
         reduce.stage(k)
@@ -479,7 +476,7 @@
         ],
         name="fetch_attend_project_reduce",
         compiler_params=pltpu.CompilerParams(
-            collective_id=0, has_side_effects=True, vmem_limit_bytes=52 << 20
+            collective_id=0, has_side_effects=True, vmem_limit_bytes=VMEM
         ),
     )(reads, visible, prefix, q, suffix, ids, w)
 

time: 107 us -> 99.1 us (0.926)
  Pallas kernels: 101 us -> 97.1 us
  local copies, waits for them, and re-layouts: 5.66 us -> 1.87 us
    pallas_call x1, Pallas kernels: 101 us -> 97.1 us  [layer(): pl.pallas_call(layer_kernel, out_shape=jax.ShapeDtypeStruct((TOK, COLS),...]
    unnamed x13 -> x1, local copies, waits for them, and re-layouts: 5.66 us -> 1.87 us
where the time goes in v3:
time: 99.1 us; the launch traced here: 98.9 us
  Pallas kernels  97.1 us (98%)
  local copies, waits for them, and re-layouts  1.87 us (2%)
    pallas_call x1, Pallas kernels, layer(): pl.pallas_call(layer_kernel, out_shape=jax.ShapeDtypeStruct((TOK, COLS),...  97.1 us

profile of v3, /device:TPU:1, one launch (start us, length us, event | category | flops | bytes accessed | tf_op | source)
XLA Modules:
  0.0 98.9 jit_solution(9615890996604101570)
XLA Ops:
  0.0 97.1 %fetch_attend_project_reduce.1 = bf16[512,512]{1,0:T(8,128)(2,1)} custom-call(s32[1,26]{1,0:T(1,128)} %reads.1, s32[1,2,26]{2,1,0:T(2,128)} %visible.1, bf16[8,64,256]{2,1,0:T(8,128)(2,1)} %prefix_hbm.1, bf16[512,1024]{1,0:T(8,128)(2,1)} %q_hbm.1, bf16[512,256]{1,0:T(8,128)(2,1)} %suffix_hbm.1, s32[1,512]{1,0:T(1,128)} %ids.1, bf16[1024,128]{1,0:T(8,128)(2,1)} %w_hbm.1), custom_call_target="tpu_custom_call" | custom-call | tf_op jit(solution)/shard_map/fetch_attend_project_reduce/pallas_call | solution.py:438
  97.1 1.9 %copy.9 = bf16[512,512]{1,0:T(8,128)(2,1)} copy(bf16[512,512]{1,0:T(8,128)(2,1)} %fetch_attend_project_reduce.1) | data formatting | bytes 1048576

commit v4 on v3

--- a/solution.py
+++ b/solution.py
@@ -260,7 +260,7 @@
         self.copy(way, k + 1, b).wait_recv()
         return way[1][k, self.rows(b), pl.ds(0, COLS // 2 if k == 3 else COLS)].astype(F32)
 
-    def stage(self, k):
+    def stage(self, k, first=0, end=NBLK):
         half = COLS // 2
 
         def body(b, _):
@@ -286,7 +286,7 @@
                     self.send(way, k, b, part)
             return 0
 
-        lax.fori_loop(0, NBLK, body, 0)
+        lax.fori_loop(first, end, body, 0)
 
     def drain(self):
         def body(b, _):
@@ -414,16 +414,23 @@
     attention.take(tiles)
     attention.score(0)
     beside = {
-        0: [(weights.across, 1)], 2: [(weights.across, 2)], 4: [(weights.across, 3)],
-        6: [(weights.last, 0)], 8: [(weights.last, 1)], 10: [(weights.last, 2)],
-        12: [(weights.last, 3)],
+        0: [(weights.across, 1)],
+        1: [(weights.across, 2)],
+        2: [(weights.across, 3)],
+        4: [(weights.last, 0)],
+        6: [(weights.last, 1)],
+        8: [(weights.last, 2)],
+        10: [(weights.last, 3)],
     }
     for i in range(4 * NBLK):
         attention.pair(i)
         for step, *j in beside.get(i, ()):
             step(*j)
-    weights.finish()
-    for k in (4, 3, 2, 1, 0):
+        if i == 11:
+            weights.finish()
+            reduce.stage(4, 0, NBLK - 1)
+    reduce.stage(4, NBLK - 1, NBLK)
+    for k in (3, 2, 1, 0):
         reduce.stage(k)
     reduce.drain()
     weights.drain()

time: 99.1 us -> 97.9 us (0.988)
  Pallas kernels: 97.1 us -> 95.9 us
    pallas_call x1, Pallas kernels: 97.1 us -> 95.9 us  [layer(): pl.pallas_call(layer_kernel, out_shape=jax.ShapeDtypeStruct((TOK, COLS),...]
where the time goes in v4:
time: 97.9 us; the launch traced here: 97.8 us
  Pallas kernels  95.9 us (98%)
  local copies, waits for them, and re-layouts  1.87 us (2%)
    pallas_call x1, Pallas kernels, layer(): pl.pallas_call(layer_kernel, out_shape=jax.ShapeDtypeStruct((TOK, COLS),...  95.9 us

profile of v4, /device:TPU:1, one launch (start us, length us, event | category | flops | bytes accessed | tf_op | source)
XLA Modules:
  0.0 97.8 jit_solution(3661589372470320058)
XLA Ops:
  0.0 95.9 %fetch_attend_project_reduce.1 = bf16[512,512]{1,0:T(8,128)(2,1)} custom-call(s32[1,26]{1,0:T(1,128)} %reads.1, s32[1,2,26]{2,1,0:T(2,128)} %visible.1, bf16[8,64,256]{2,1,0:T(8,128)(2,1)} %prefix_hbm.1, bf16[512,1024]{1,0:T(8,128)(2,1)} %q_hbm.1, bf16[512,256]{1,0:T(8,128)(2,1)} %suffix_hbm.1, s32[1,512]{1,0:T(1,128)} %ids.1, bf16[1024,128]{1,0:T(8,128)(2,1)} %w_hbm.1), custom_call_target="tpu_custom_call" | custom-call | tf_op jit(solution)/shard_map/fetch_attend_project_reduce/pallas_call | solution.py:445
  95.9 1.9 %copy.9 = bf16[512,512]{1,0:T(8,128)(2,1)} copy(bf16[512,512]{1,0:T(8,128)(2,1)} %fetch_attend_project_reduce.1) | data formatting | bytes 1048576

commit v5 on v4

--- a/solution.py
+++ b/solution.py
@@ -429,8 +429,11 @@
         if i == 11:
             weights.finish()
             reduce.stage(4, 0, NBLK - 1)
+        if i == 13:
+            reduce.stage(3, 0, 2)
     reduce.stage(4, NBLK - 1, NBLK)
-    for k in (3, 2, 1, 0):
+    reduce.stage(3, 2, NBLK)
+    for k in (2, 1, 0):
         reduce.stage(k)
     reduce.drain()
     weights.drain()

time: 97.9 us -> 97.9 us (level)
  no operation moved by 1% of the time
where the time goes in v5:
time: 97.9 us; the launch traced here: 97.8 us
  Pallas kernels  95.9 us (98%)
  local copies, waits for them, and re-layouts  1.87 us (2%)
    pallas_call x1, Pallas kernels, layer(): pl.pallas_call(layer_kernel, out_shape=jax.ShapeDtypeStruct((TOK, COLS),...  95.9 us

profile of v5, /device:TPU:1, one launch (start us, length us, event | category | flops | bytes accessed | tf_op | source)
XLA Modules:
  0.0 97.8 jit_solution(4007868038541052373)
XLA Ops:
  0.0 95.9 %fetch_attend_project_reduce.1 = bf16[512,512]{1,0:T(8,128)(2,1)} custom-call(s32[1,26]{1,0:T(1,128)} %reads.1, s32[1,2,26]{2,1,0:T(2,128)} %visible.1, bf16[8,64,256]{2,1,0:T(8,128)(2,1)} %prefix_hbm.1, bf16[512,1024]{1,0:T(8,128)(2,1)} %q_hbm.1, bf16[512,256]{1,0:T(8,128)(2,1)} %suffix_hbm.1, s32[1,512]{1,0:T(1,128)} %ids.1, bf16[1024,128]{1,0:T(8,128)(2,1)} %w_hbm.1), custom_call_target="tpu_custom_call" | custom-call | tf_op jit(solution)/shard_map/fetch_attend_project_reduce/pallas_call | solution.py:448
  95.9 1.9 %copy.9 = bf16[512,512]{1,0:T(8,128)(2,1)} copy(bf16[512,512]{1,0:T(8,128)(2,1)} %fetch_attend_project_reduce.1) | data formatting | bytes 1048576

commit v6 on v5

--- a/solution.py
+++ b/solution.py
@@ -46,6 +46,11 @@
     )
 
 
+def far_first(k):
+    x, y = k // 8, k // 2 % 4
+    return -min(x, 4 - x) - min(y, 4 - y), k * 11 % GROUPS
+
+
 class Tiles:
     def __init__(self, reads, prefix, ask, table, asked, packed, got, hot_out, hot_recv,
                  sem_send, sem_recv, spread_send, spread_recv, local_sem):
@@ -56,7 +61,7 @@
         self.x, self.y, self.c, self.z = coords()
         self.me = lax.axis_index("dp")
         self.peers = [place(self.x + k // 8, self.y + (k // 2) % 4, self.c + k % 2)
-                      for k in range(1, GROUPS)]
+                      for k in sorted(range(1, GROUPS), key=far_first)]
 
     def plan(self):
         lane = lax.broadcasted_iota(jnp.int32, (1, 128), 1)

time: 97.9 us -> 97.7 us (level)
  no operation moved by 1% of the time
where the time goes in v6:
time: 97.7 us; the launch traced here: 97.5 us
  Pallas kernels  95.6 us (98%)
  local copies, waits for them, and re-layouts  1.87 us (2%)
    pallas_call x1, Pallas kernels, layer(): pl.pallas_call(layer_kernel, out_shape=jax.ShapeDtypeStruct((TOK, COLS),...  95.6 us

profile of v6, /device:TPU:1, one launch (start us, length us, event | category | flops | bytes accessed | tf_op | source)
XLA Modules:
  0.0 97.5 jit_solution(11439483523099555941)
XLA Ops:
  0.0 95.6 %fetch_attend_project_reduce.1 = bf16[512,512]{1,0:T(8,128)(2,1)} custom-call(s32[1,26]{1,0:T(1,128)} %reads.1, s32[1,2,26]{2,1,0:T(2,128)} %visible.1, bf16[8,64,256]{2,1,0:T(8,128)(2,1)} %prefix_hbm.1, bf16[512,1024]{1,0:T(8,128)(2,1)} %q_hbm.1, bf16[512,256]{1,0:T(8,128)(2,1)} %suffix_hbm.1, s32[1,512]{1,0:T(1,128)} %ids.1, bf16[1024,128]{1,0:T(8,128)(2,1)} %w_hbm.1), custom_call_target="tpu_custom_call" | custom-call | tf_op jit(solution)/shard_map/fetch_attend_project_reduce/pallas_call | solution.py:453
  95.6 1.9 %copy.9 = bf16[512,512]{1,0:T(8,128)(2,1)} copy(bf16[512,512]{1,0:T(8,128)(2,1)} %fetch_attend_project_reduce.1) | data formatting | bytes 1048576
